TPU v7x, 256 devices: a whole 4x4x8 slice. The times are simulated.
256 devices in a mesh: role: 2 (over x_lo), fsdp: 16 (over z, core), dp: 8 (over y, x_hi).
Axes of the slice: x: 4 (x_hi: 2, x_lo: 2; x = x_hi * 2 + x_lo), y: 4, z: 8, core: 2. Of those that a mesh axis runs over, the one named last changes fastest.
Arguments:
- acts: bfloat16 [4096, 4096], P(('role', 'fsdp'), 'dp'), may hold values from -6 to 6
- cotangent: bfloat16 [4096, 16384], P('dp', ('role', 'fsdp')), may hold values from -6 to 6
- example_of: int32 [4096, 1], P('dp'), may hold values from 0 to 127
- stats_old: float32 [8, 32, 2, 512, 512], P('dp', ('role', 'fsdp')), may hold values from -2 to 4096, as said below
- stale_roots: float32 [8, 16, 2, 512, 512], P('dp', 'fsdp'), may hold values from -1 to 1, as said below
Outputs:
- update: float32 [4096, 16384], P('dp', ('role', 'fsdp'))
- new_stats: float32 [8, 32, 2, 512, 512], P('dp', ('role', 'fsdp'))
Inputs may be any that keep to these rules, and one draw needn't show every extreme that they name: `example_of`: every example 0 .. 127 is named by at least one token. Each 512 x 512 matrix stats_old[i, j, k] is symmetric and positive definite. Each 512 x 512 matrix stale_roots[i, j, k] is symmetric and positive definite.
All inputs are finite; a program needn't handle non-finite values.
Results may differ from a plain program's by a relative error of at most 0.0028.
Values may be sent and summed in bfloat16 or wider, within the bound.
A program may use at most 128 MiB of HBM per device.

v0:
```python
import jax
import jax.numpy as jnp
from jax import lax
from jax.sharding import PartitionSpec as P

B = 512
NEWTON = 3
T_DP = 512


decay = 0.9
highest = lax.Precision.HIGHEST


def shifted(value, axis, steps):
    count = lax.axis_size(axis)
    leading, last = (max(0, -steps), min(count, count - steps))
    return lax.ppermute(value, axis, [(source, source + steps) for source in range(leading, last)])


def inverse_root(matrix):
    identity = jnp.eye(matrix.shape[-1], dtype=jnp.float32)
    scale = jnp.sqrt(jnp.sum(matrix * matrix, axis=(-2, -1), keepdims=True))
    current = matrix / scale
    root = identity * scale ** (-0.25)
    for iteration in range(NEWTON):
        factor = (5.0 * identity - current) * 0.25
        root = jnp.einsum("ijab,ijbc->ijac", root, factor, precision=highest)
        if iteration + 1 < NEWTON:
            square = jnp.einsum("ijab,ijbc->ijac", factor, factor, precision=highest)
            fourth = jnp.einsum("ijab,ijbc->ijac", square, square, precision=highest)
            current = jnp.einsum("ijab,ijbc->ijac", fourth, current, precision=highest)
    return root


def contract_rows(left_rows, right_rows):
    return lax.dot_general(
        left_rows, right_rows, (((0,), (0,)), ((), ())), preferred_element_type=jnp.float32
    )


def shards(acts, cotangent, example_of, stats_old, stale_roots):
    group_index = lax.axis_index("role")
    example_total = T_DP // 32 * lax.axis_size("dp")
    labels = jnp.arange(example_total, dtype=jnp.int32)
    onehot = (example_of[:, 0][:, None] == labels[None, :]).astype(jnp.float32)
    counts = lax.psum(jnp.sum(onehot, axis=0), "dp")
    weight = jnp.sum(onehot * (1.0 / counts)[None, :], axis=1)
    scaled = (cotangent.astype(jnp.float32) * weight[:, None]).astype(jnp.bfloat16)
    scaled_all = lax.all_gather(scaled, "dp", axis=0, tiled=True)
    width = scaled.shape[1]
    height = acts.shape[1]
    partner = shifted(scaled_all, "role", -1)
    joined = jnp.concatenate([scaled_all, partner], axis=1)
    total = jnp.zeros((height, 2 * width), jnp.float32)
    piece = lax.all_gather(acts, ("role", "fsdp"), axis=0, tiled=True)
    paired = lax.cond(group_index == 0, lambda: contract_rows(piece, joined), lambda: total)
    handed = shifted(paired[:, width:], "role", 1)
    grad = jnp.where(group_index == 0, paired[:, :width], handed)
    row_blocks = height // B
    col_blocks = width // B
    blocks = grad.reshape(row_blocks, B, col_blocks, B).transpose(0, 2, 1, 3)
    left = decay * stats_old[:, :, 0] + (1.0 - decay) * jnp.einsum(
        "ijab,ijcb->ijac", blocks, blocks, precision=highest
    )
    right = decay * stats_old[:, :, 1] + (1.0 - decay) * jnp.einsum(
        "ijba,ijbc->ijac", blocks, blocks, precision=highest
    )
    new_stats = jnp.stack([left, right], axis=2)
    root_left, root_right = lax.cond(
        group_index == 1,
        lambda: (inverse_root(left), inverse_root(right)),
        lambda: (stale_roots[:, :, 0], stale_roots[:, :, 1]),
    )
    inner = jnp.einsum("ijab,ijbc->ijac", root_left, blocks, precision=highest)
    product = jnp.einsum("ijab,ijbc->ijac", inner, root_right, precision=highest)
    grad_size = jnp.sqrt(jnp.mean(blocks * blocks, axis=(2, 3)))
    prod_size = jnp.sqrt(jnp.mean(product * product, axis=(2, 3)) + 1e-06)
    update_blocks = product * (grad_size / prod_size)[:, :, None, None]
    update = update_blocks.transpose(0, 2, 1, 3).reshape(height, width)
    return (update, new_stats)


def solution(mesh):
    return jax.shard_map(
        shards,
        mesh=mesh,
        in_specs=(
            P(("role", "fsdp"), "dp"),
            P("dp", ("role", "fsdp")),
            P("dp", None),
            P("dp", ("role", "fsdp"), None, None, None),
            P("dp", "fsdp", None, None, None),
        ),
        out_specs=(P("dp", ("role", "fsdp")), P("dp", ("role", "fsdp"), None, None, None)),
        check_vma=False,
    )
```

profile of v0, /device:TPU:2, one launch (start us, length us, event | category | flops | bytes accessed | tf_op | source)
XLA Modules:
  0.0 339.4 jit_solution(7369805681953358825)
XLA Ops:
  8.0 23.6 %psum.7 = f32[128]{0:T(128)S(1)} all-reduce(f32[128]{0:T(128)S(1)} %convert_reduce_fusion), channel_id=1, replica_groups=mesh['role'=2,'fsdp'=16,'dp'=8] {'dp'}, use_global_device_ids=true, to_apply=%region_1.0 | all-reduce | flops 128 | bytes 1024 | tf_op jit(solution)/shard_map/psum | solution.py:47
  32.6 2.0 multiply_convert_fusion
  35.4 73.7 %all-gather.5.cloned.1.call-done = bf16[4096,512]{1,0:T(8,128)(2,1)} async-done(((bf16[512,512]{1,0:T(8,128)(2,1)}), bf16[4096,512]{1,0:T(8,128)(2,1)}) %all-gather.5.cloned.1.call-update) | async-done | bytes 4194320 | tf_op jit(solution)/shard_map/all_gather | solution.py:50
  109.1 5.3 %collective-permute-start = (bf16[4096,512]{1,0:T(8,128)(2,1)}, bf16[4096,512]{1,0:T(8,128)(2,1)}, u32[]{:S(2)}, u32[]{:S(2)}) collective-permute-start(bf16[4096,512]{1,0:T(8,128)(2,1)} %all-gather.5.cloned.1.call-done), channel_id=1, source_target_pairs={{128,0},{129,1},{130,2},{131,3},{132,4},{133,5},{134,6},{135,7},{1... | collective-permute-start | bytes 12582920 | tf_op jit(solution)/shard_map/ppermute | solution.py:18
  114.4 108.8 %collective-permute-done = bf16[4096,512]{1,0:T(8,128)(2,1)} collective-permute-done((bf16[4096,512]{1,0:T(8,128)(2,1)}, bf16[4096,512]{1,0:T(8,128)(2,1)}, u32[]{:S(2)}, u32[]{:S(2)}) %collective-permute-start) | collective-permute-done | bytes 4194336 | tf_op jit(solution)/shard_map/ppermute | solution.py:18
  223.2 7.9 %pad_maximum_fusion = bf16[4096,1024]{1,0:T(8,128)(2,1)} fusion(bf16[4096,512]{1,0:T(8,128)(2,1)} %collective-permute-done, bf16[4096,512]{1,0:T(8,128)(2,1)} %all-gather.5.cloned.1.call-done), kind=kLoop, calls=%fused_computation.81 | loop fusion | flops 16777216 | bytes 16777216 | tf_op jit(solution)/shard_map/concatenate | solution.py:54
  232.8 32.3 %collective-permute-done.1 = f32[512,512]{1,0:T(8,128)} collective-permute-done((f32[512,512]{1,0:T(8,128)S(1)}, f32[512,512]{1,0:T(8,128)}, u32[]{:S(2)}, u32[]{:S(2)}) %collective-permute-start.1) | collective-permute-done | bytes 1048608 | tf_op jit(solution)/shard_map/ppermute | solution.py:18
  265.1 2.2 multiply_reduce_fusion.3
  267.3 3.3 fusion.76
  270.5 2.9 fusion.77
  273.4 46.8 %conditional.3 = (f32[512,512]{1,0:T(8,128)}, f32[512,512]{1,0:T(8,128)}) conditional(s32[]{:T(128)} %convert_element_type.21, (f32[1,1,2,512,512]{4,3,2,1,0:T(8,128)S(1)}) %tuple.43, (f32[512,512]{1,0:T(8,128)}, f32[512,512]{1,0:T(8,128)S(1)}) %tuple.28), branch_computations={%region_5.6_spmd, %region_6.9_spmd} | conditional | flops 29005185024 | bytes 56623256 | solution.py:70
  273.9 2.1 multiply_reduce_fusion
  276.7 2.0 fusion.14
  286.2 2.8 fusion.1
  291.0 2.1 fusion.12
  293.1 2.8 fusion.84
  296.7 3.6 %fusion.21 = f32[512,512]{1,0:T(8,128)S(1)} fusion(f32[512,512]{1,0:T(8,128)} %get-tuple-element.18, f32[]{:T(128)S(6)} %sqrt.11), kind=kOutput, calls=%fused_computation.26 | convolution fusion | flops 1611923456 | bytes 2097156 | tf_op jit(solution)/shard_map/cond/branch_1_fun/ijab,ijbc->ijac/dot_general | solution.py:30
  302.1 3.1 fusion.74
  309.0 3.1 fusion
  312.1 3.2 fusion.8
  317.2 2.8 fusion.81
  320.3 3.1 fusion.85
  323.4 3.8 %multiply_reduce_fusion.2 = (f32[]{:T(128)}, f32[512,512]{1,0:T(8,128)S(1)}) fusion(f32[512,512]{1,0:T(8,128)S(1)} %fusion.85, f32[512,512]{1,0:T(8,128)} %get-tuple-element.25), kind=kOutput, calls=%fused_computation.88 | convolution fusion | flops 1611137024 | bytes 3145732 | tf_op jit(solution)/shard_map/ijab,ijbc->ijac/dot_general | solution.py:76
  329.6 2.7 pad_maximum_fusion.1
  (30 shorter events, 22.4 us)
Async XLA Ops:
  7.2 101.9 %all-gather.5.cloned.1.call-start = ((), (), s32[]{:S(2)}) async-start(), calls=%async_computation.1 | async-start | bytes 4718592 | tf_op jit(solution)/shard_map/all_gather | solution.py:50
  34.6 196.5 %all-gather.3.cloned.1.call-start = ((), (), s32[]{:S(2)}) async-start(), calls=%async_computation | async-start | bytes 4325376 | tf_op jit(solution)/shard_map/all_gather | solution.py:56
  109.1 114.1 %collective-permute-start = (bf16[4096,512]{1,0:T(8,128)(2,1)}, bf16[4096,512]{1,0:T(8,128)(2,1)}, u32[]{:S(2)}, u32[]{:S(2)}) collective-permute-start(bf16[4096,512]{1,0:T(8,128)(2,1)} %all-gather.5.cloned.1.call-done), channel_id=1, source_target_pairs={{128,0},{129,1},{130,2},{131,3},{132,4},{133,5},{134,6},{135,7},{1... | collective-permute-start | bytes 12582920 | tf_op jit(solution)/shard_map/ppermute | solution.py:18
  231.4 33.6 %collective-permute-start.1 = (f32[512,512]{1,0:T(8,128)S(1)}, f32[512,512]{1,0:T(8,128)}, u32[]{:S(2)}, u32[]{:S(2)}) collective-permute-start(f32[512,512]{1,0:T(8,128)S(1)} %slice.23), channel_id=1, source_target_pairs={{0,128},{1,129},{2,130},{3,131},{4,132},{5,133},{6,134},{7,135},{8... | collective-permute-start | bytes 3145736 | tf_op jit(solution)/shard_map/ppermute | solution.py:18
  232.8 37.8 %copy-start.3 = (f32[1,1,2,512,512]{4,3,2,1,0:T(8,128)S(1)}, f32[1,1,2,512,512]{4,3,2,1,0:T(8,128)}, u32[]{:S(2)}) copy-start(f32[1,1,2,512,512]{4,3,2,1,0:T(8,128)} %param.12) | copy-start | bytes 6291460
  267.3 6.2 %copy-start.2 = (f32[1,1,2,512,512]{4,3,2,1,0:T(8,128)S(1)}, f32[1,1,2,512,512]{4,3,2,1,0:T(8,128)}, u32[]{:S(2)}) copy-start(f32[1,1,2,512,512]{4,3,2,1,0:T(8,128)} %param.13) | copy-start | bytes 6291460
  289.1 4.0 %copy-start.1 = (f32[512,512]{1,0:T(8,128)S(1)}, f32[512,512]{1,0:T(8,128)}, u32[]{:S(2)}) copy-start(f32[512,512]{1,0:T(8,128)} %fusion.1) | copy-start | bytes 3145732 | tf_op jit(solution)/shard_map/cond
  312.1 5.1 %copy-start = (f32[512,512]{1,0:T(8,128)S(1)}, f32[512,512]{1,0:T(8,128)}, u32[]{:S(2)}) copy-start(f32[512,512]{1,0:T(8,128)} %fusion) | copy-start | bytes 3145732 | tf_op jit(solution)/shard_map/cond
Sparse Core Ops, SparseCore 0:
  34.7 74.3 all-gather.4
  110.9 64.9 all-gather.2
where the time goes:
time: 346 us; the launch traced here: 339 us
  waiting for transfers between devices  216 us (62%)
  matrix products  55.4 us (16%)
  blocking collectives  23.6 us (7%)
  other arithmetic  19.6 us (6%)
  between operations  15.7 us (5%)
  starting transfers between devices  6.67 us (2%)
    ppermute x2, waiting for transfers between devices, shifted(): lax.ppermute(value, axis, [(source, source + steps) for source in range(l...  141 us
    all_gather x1, waiting for transfers between devices, shards(): scaled_all = lax.all_gather(scaled, 'dp', axis=0, tiled=True)  73.7 us
    psum x1, blocking collectives, shards(): counts = lax.psum(jnp.sum(onehot, axis=0), 'dp')  23.6 us
    dot_general x6, matrix products, inverse_root(): root = jnp.einsum('ijab,ijbc->ijac', root, factor, precision=highest)  14.8 us
    dot_general x4, matrix products, inverse_root(): current = jnp.einsum('ijab,ijbc->ijac', fourth, current, precision=highest)  10.8 us
    dot_general x4, matrix products, inverse_root(): square = jnp.einsum('ijab,ijbc->ijac', factor, factor, precision=highest)  9.39 us
    concatenate x1, other arithmetic, shards(): joined = jnp.concatenate([scaled_all, partner], axis=1)  7.86 us
    dot_general x4, matrix products, inverse_root(): fourth = jnp.einsum('ijab,ijbc->ijac', square, square, precision=highest)  7.36 us
  transfers between devices with their start and end apart: 4, of which 3 were waited for; matrix products, arithmetic and copies ran while one was open for 2% of the time, Pallas kernels for 0%

commit v1 on v0

v1 whole, which is shorter than its diff:
```python
import functools

import jax
import jax.numpy as jnp
from jax import lax
from jax.experimental import pallas as pl
from jax.experimental.pallas import tpu as pltpu
from jax.sharding import PartitionSpec as P

MESH = pl.DeviceIdType.MESH
F32 = jnp.float32
BF16 = jnp.bfloat16
B = 512
Q = 128
EXAMPLES = 128
MIB = 1 << 20


def contract(left, right, left_dim, right_dim):
    return lax.dot_general(
        left, right, (((left_dim,), (right_dim,)), ((), ())), preferred_element_type=F32
    )


class Names:
    def __init__(self):
        self.table = {}

    def __call__(self, *key):
        return self.table.setdefault(key, len(self.table))


COPIES = 96


def gather_kernel(
    acts_ref, cot_ref, ids_ref, grad_ref, acts_all, cot_all, ids_all, weights, local_sem, send_sem, recv_sem
):
    role = lax.axis_index("role")
    fsdp = lax.axis_index("fsdp")
    dp = lax.axis_index("dp")
    z, core = fsdp // 2, fsdp % 2
    y, half = dp // 2, dp % 2
    number = Names()

    def device(role=role, z=z, core=core, y=y, half=half):
        return (role, z * 2 + core, y * 2 + half)

    across = device(half=1 - half)
    y_up, y_down = device(y=(y + 1) % 4), device(y=(y + 3) % 4)
    z_up, z_down = device(z=(z + 1) % 8), device(z=(z + 7) % 8)
    partner = device(role=1 - role)
    sibling = device(core=1 - core)
    row_peers = [(role, fsdp, (dp + step) % 8) for step in range(1, 8)]

    def acts_block(block_role, block_z, block_core):
        index = block_role * 16 + block_z * 2 + block_core
        return acts_all.at[index // 4, pl.ds(pl.multiple_of((index % 4) * Q, Q), Q)]

    def cot_part(block_y, block_half, quarter):
        return cot_all.at[block_y * 2 + block_half, pl.ds(quarter * Q, Q)]

    sent = []

    def send(ref, key, target):
        index = number(*key)
        copy = pltpu.make_async_remote_copy(
            src_ref=ref,
            dst_ref=ref,
            send_sem=send_sem.at[index],
            recv_sem=recv_sem.at[index],
            device_id=target,
            device_id_type=MESH,
        )
        copy.start()
        sent.append(copy)

    def arrived(ref, key):
        index = number(*key)
        pltpu.make_async_remote_copy(
            src_ref=ref,
            dst_ref=ref,
            send_sem=send_sem.at[index],
            recv_sem=recv_sem.at[index],
            device_id=sibling,
            device_id_type=MESH,
        ).wait_recv()

    own_acts = acts_block(role, z, core)
    own_cot = cot_all.at[dp]
    local = [
        pltpu.make_async_copy(ids_ref, ids_all.at[dp], local_sem.at[0]),
        pltpu.make_async_copy(acts_ref, own_acts, local_sem.at[1]),
        pltpu.make_async_copy(cot_ref, own_cot, local_sem.at[2]),
    ]
    for copy in local:
        copy.start()

    barrier = pltpu.get_barrier_semaphore()
    others = [y_up, y_down, across] + [
        device(y=(y + 1) % 4, half=1 - half),
        device(y=(y + 3) % 4, half=1 - half),
        device(y=(y + 2) % 4),
        device(y=(y + 2) % 4, half=1 - half),
    ]
    everyone = others + [z_up, z_down, partner, sibling]
    for target in everyone:
        pl.semaphore_signal(barrier, inc=1, device_id=target, device_id_type=MESH)
    for copy in local:
        copy.wait()
    pl.semaphore_wait(barrier, len(everyone))

    for step, target in enumerate(row_peers, 1):
        send(ids_all.at[dp], ("ids", step), target)
    send(own_acts, ("partner",), partner)
    send(own_acts, ("up", 0, 1), z_up)
    send(own_acts, ("down", 0, 1), z_down)

    def own(quarter, direction):
        send(cot_part(y, half, quarter), ("y", direction, 0, quarter), y_up if direction else y_down)

    own(0, 1)
    own(3, 0)
    for quarter in (0, 3):
        send(cot_part(y, half, quarter), ("x", 0, quarter), across)
    own(1, 1)
    own(2, 0)
    for quarter in (1, 2):
        send(cot_part(y, half, quarter), ("x", 0, quarter), across)
    own(2, 1)
    own(1, 0)
    send(own_acts, ("sibling", 0, 0), sibling)

    for step in range(1, 8):
        arrived(ids_all.at[(dp + 8 - step) % 8], ("ids", step))

    def onehot(block):
        labels = lax.broadcasted_iota(jnp.int32, (EXAMPLES, B), 0)
        return jnp.where(ids_all[block] == labels, 1.0, 0.0)

    seen = onehot(0)
    for block in range(1, 8):
        seen += onehot(block)
    inverse = jnp.broadcast_to(1.0 / jnp.sum(seen, axis=1, keepdims=True), (EXAMPLES, Q))
    high = inverse.astype(BF16)
    rest = inverse - high.astype(F32)
    middle = rest.astype(BF16)
    low = (rest - middle.astype(F32)).astype(BF16)
    split = jnp.concatenate([high, middle, low], axis=1)

    def weigh(block):
        spread = contract(onehot(block).astype(BF16), split, 0, 0)
        weights[block] = (spread[:, :Q] + spread[:, Q : 2 * Q]) + spread[:, 2 * Q :]

    def step_acts(stream, hop, last=False):
        stream_role = role if stream == 0 else 1 - role
        for key, sign, target in (("up", -1, z_up), ("down", 1, z_down)):
            if hop == 4 and stream != (0 if key == "up" else 1):
                continue
            block = acts_block(stream_role, (z + 8 + sign * hop) % 8, core)
            arrived(block, (key, stream, hop))
            if hop < 3 or (hop == 3 and stream == (0 if key == "up" else 1)):
                send(block, (key, stream, hop + 1), target)
            send(block, ("sibling", stream, (8 + sign * hop) % 8), sibling)

    block = acts_block(1 - role, z, core)
    arrived(block, ("partner",))
    send(block, ("up", 1, 1), z_up)
    send(block, ("down", 1, 1), z_down)
    send(block, ("sibling", 1, 0), sibling)
    step_acts(0, 1)

    up_y, down_y, far_y = (y + 1) % 4, (y + 3) % 4, (y + 2) % 4
    for first, second in ((0, 3), (1, 2)):
        part = cot_part(down_y, half, first)
        arrived(part, ("y", 1, 0, first))
        send(part, ("y", 1, 1, first), y_up)
        part = cot_part(up_y, half, second)
        arrived(part, ("y", 0, 0, second))
        send(part, ("y", 0, 1, second), y_down)
    own(3, 1)
    own(0, 0)

    step_acts(1, 1)
    step_acts(0, 2)
    for quarter in (0, 3, 1, 2):
        part = cot_part(y, 1 - half, quarter)
        arrived(part, ("x", 0, quarter))
        send(part, ("y", 1, 2, quarter), y_up)
        send(part, ("y", 0, 2, quarter), y_down)
    step_acts(1, 2)
    for quarters in ((0, 3), (1, 2)):
        for quarter in quarters:
            part = cot_part(far_y, half, quarter)
            arrived(part, ("y", 1 if quarter < 2 else 0, 1, quarter))
            send(part, ("x", 1, quarter), across)
    step_acts(0, 3)
    step_acts(1, 3)

    for block in range(8):
        weigh(block)

    for quarter in (2, 3):
        arrived(cot_part(down_y, half, quarter), ("y", 1, 0, quarter))
    for quarter in (0, 1):
        arrived(cot_part(up_y, half, quarter), ("y", 0, 0, quarter))
    step_acts(0, 4)
    step_acts(1, 4)
    for stream in range(2):
        stream_role = role if stream == 0 else 1 - role
        for offset in range(8):
            arrived(acts_block(stream_role, (z + offset) % 8, 1 - core), ("sibling", stream, offset))

    def product(block, start, size):
        rows = pl.ds(start, size)
        weight = weights[block, rows]
        scaled = jnp.concatenate(
            [
                (cot_all[block, rows, pl.ds(lane, Q)].astype(F32) * weight).astype(BF16)
                for lane in range(0, B, Q)
            ],
            axis=1,
        )
        return contract(acts_all[block, rows], scaled, 0, 0)

    grad_ref[...] = product(dp, 0, B)
    for block in (down_y * 2 + half, up_y * 2 + half, y * 2 + 1 - half, far_y * 2 + half):
        grad_ref[...] += product(block, 0, B)
    for quarters, start in (((0, 3), None), ((1, 2), None)):
        for quarter in quarters:
            arrived(cot_part(down_y, 1 - half, quarter), ("y", 1, 2, quarter))
            grad_ref[...] += product(down_y * 2 + 1 - half, quarter * Q, Q)
            arrived(cot_part(up_y, 1 - half, quarter), ("y", 0, 2, quarter))
            grad_ref[...] += product(up_y * 2 + 1 - half, quarter * Q, Q)
            arrived(cot_part(far_y, 1 - half, quarter), ("x", 1, quarter))
            grad_ref[...] += product(far_y * 2 + 1 - half, quarter * Q, Q)

    for copy in sent:
        copy.wait_send()
    assert len(number.table) <= COPIES


def gather(acts, cotangent, ids):
    return pl.pallas_call(
        gather_kernel,
        out_shape=jax.ShapeDtypeStruct((B, B), F32),
        in_specs=[pl.BlockSpec(memory_space=pl.ANY)] * 3,
        out_specs=pl.BlockSpec(memory_space=pltpu.VMEM),
        scratch_shapes=[
            pltpu.VMEM((8, B, B), BF16),
            pltpu.VMEM((8, B, B), BF16),
            pltpu.VMEM((8, 1, B), jnp.int32),
            pltpu.VMEM((8, B, Q), F32),
            pltpu.SemaphoreType.DMA((3,)),
            pltpu.SemaphoreType.DMA((COPIES,)),
            pltpu.SemaphoreType.DMA((COPIES,)),
        ],
        compiler_params=pltpu.CompilerParams(
            collective_id=0, has_side_effects=True, vmem_limit_bytes=24 * MIB
        ),
    )(acts, cotangent, ids)


def parts_of(matrix):
    high = matrix.astype(BF16)
    return high, (matrix - high.astype(F32)).astype(BF16)


def precise(left, right, left_dim, right_dim):
    (left_high, left_low), (right_high, right_low) = left, right
    return contract(
        jnp.concatenate([left_high, left_low, left_high], axis=left_dim),
        jnp.concatenate([right_high, right_high, right_low], axis=right_dim),
        left_dim,
        right_dim,
    )


def rough(left, right):
    return contract(left.astype(BF16), right.astype(BF16), 1, 0)


def total(matrix):
    return jnp.sum(jnp.sum(matrix, axis=0, keepdims=True), axis=1, keepdims=True)


def block_kernel(
    grad_ref, stats_ref, stale_ref, update_ref, new_ref, grad, stats, stale, fresh, update, apart, load_sem, store_sem
):
    role = lax.axis_index("role")
    loads = [
        pltpu.make_async_copy(grad_ref, grad, load_sem.at[0]),
        pltpu.make_async_copy(stats_ref.at[0, 0, 0], stats.at[0], load_sem.at[1]),
        pltpu.make_async_copy(stats_ref.at[0, 0, 1], stats.at[1], load_sem.at[2]),
    ]
    for copy in loads:
        copy.start()
    stale_load = pltpu.make_async_copy(stale_ref.at[0, 0], stale, load_sem.at[3])
    stale_load.start()
    stores = [
        pltpu.make_async_copy(fresh.at[0], new_ref.at[0, 0, 0], store_sem.at[0]),
        pltpu.make_async_copy(fresh.at[1], new_ref.at[0, 0, 1], store_sem.at[1]),
    ]
    loads[0].wait()
    halves = parts_of(grad[...])
    for side in range(2):
        gram = precise(halves, halves, 1 - side, 1 - side)
        loads[1 + side].wait()
        fresh[side] = 0.9 * stats[side] + (1.0 - 0.9) * gram
        stores[side].start()
    stale_load.wait()

    @pl.when(role == 0)
    def _():
        inner = precise(parts_of(stale[0]), halves, 1, 0)
        update[...] = precise(parts_of(inner), parts_of(stale[1]), 1, 0)

    @pl.when(role == 1)
    def _():
        square = [total(fresh[side] * fresh[side]) for side in range(2)]
        stats[0] = fresh[0] * lax.rsqrt(square[0])
        stats[1] = fresh[1] * lax.rsqrt(square[1])
        for side in range(2):
            m = stats[side]
            m2 = rough(m, m)
            m3 = rough(m, m2)
            n = (625.0 / 256) * m - (500.0 / 256) * m2 + (150.0 / 256) * m3
            n += rough(m3, (1.0 / 256) * m2 - (20.0 / 256) * m)
            n2 = rough(n, n)
            n3 = rough(n, n2)
            g = (-5.0 / 16 - 3125.0 / 4096) * n + (3125.0 / 4096) * n2 - (1250.0 / 4096) * n3
            g += rough(n3, (250.0 / 4096) * n - (25.0 / 4096) * n2 + (1.0 / 4096) * n3)
            apart[side] = 1.25 * g - (25.0 / 64) * m - 0.25 * rough(m, g)
        scale = [lax.rsqrt(jnp.sqrt(jnp.sqrt(value))) for value in square]
        whole = grad[...]
        inner = (125.0 / 64) * whole + rough(apart[0], whole)
        product = (125.0 / 64) * inner + rough(inner, apart[1])
        update[...] = product * (scale[0] * scale[1])

    whole = grad[...]
    grad_size = jnp.sqrt(total(whole * whole) * (1.0 / (B * B)))
    product = update[...]
    prod_size = jnp.sqrt(total(product * product) * (1.0 / (B * B)) + 1e-06)
    update[...] = product * (grad_size / prod_size)
    last = pltpu.make_async_copy(update, update_ref, store_sem.at[2])
    last.start()
    for copy in stores:
        copy.wait()
    last.wait()


def block_step(grad, stats_old, stale_roots):
    return pl.pallas_call(
        block_kernel,
        out_shape=(
            jax.ShapeDtypeStruct((B, B), F32),
            jax.ShapeDtypeStruct((1, 1, 2, B, B), F32),
        ),
        in_specs=[pl.BlockSpec(memory_space=pl.ANY)] * 3,
        out_specs=(pl.BlockSpec(memory_space=pl.ANY),) * 2,
        scratch_shapes=[
            pltpu.VMEM((B, B), F32),
            pltpu.VMEM((2, B, B), F32),
            pltpu.VMEM((2, B, B), F32),
            pltpu.VMEM((2, B, B), F32),
            pltpu.VMEM((B, B), F32),
            pltpu.VMEM((2, B, B), F32),
            pltpu.SemaphoreType.DMA((4,)),
            pltpu.SemaphoreType.DMA((3,)),
        ],
        compiler_params=pltpu.CompilerParams(vmem_limit_bytes=32 * MIB),
    )(grad, stats_old, stale_roots)


def shards(acts, cotangent, example_of, stats_old, stale_roots):
    grad = gather(acts, cotangent, example_of.reshape(1, B))
    return block_step(grad, stats_old, stale_roots)


def solution(mesh):
    return jax.shard_map(
        shards,
        mesh=mesh,
        in_specs=(
            P(("role", "fsdp"), "dp"),
            P("dp", ("role", "fsdp")),
            P("dp", None),
            P("dp", ("role", "fsdp"), None, None, None),
            P("dp", "fsdp", None, None, None),
        ),
        out_specs=(P("dp", ("role", "fsdp")), P("dp", ("role", "fsdp"), None, None, None)),
        check_vma=False,
    )
```

time: 346 us -> 58.5 us (0.17)
  the two profiles are of different devices: /device:TPU:2 before, /device:TPU:3 now
where the time goes in v1:
time: 58.5 us; the launch traced here: 58.3 us
  Pallas kernels  51.7 us (88%)
  local copies, waits for them, and re-layouts  5.8 us (10%)
  between operations  0.82 us (1%)
    pallas_call x1, Pallas kernels, gather(): pl.pallas_call(gather_kernel, out_shape=jax.ShapeDtypeStruct((B, B), F32)...  41.6 us
    pallas_call x1, Pallas kernels, block_step(): pl.pallas_call(block_kernel, out_shape=(jax.ShapeDtypeStruct((B, B), F32)...  10.1 us
    unnamed x10, local copies, waits for them, and re-layouts  5.8 us

profile of v1, /device:TPU:3, one launch (start us, length us, event | category | flops | bytes accessed | tf_op | source)
XLA Modules:
  0.0 58.3 jit_solution(5148333744463946576)
XLA Ops:
  0.6 0.0 copy-start.2
  0.6 1.0 %copy-done.2 = bf16[512,512]{1,0:T(8,128)(2,1)S(1)} copy-done((bf16[512,512]{1,0:T(8,128)(2,1)S(1)}, bf16[512,512]{1,0:T(8,128)(2,1)}, u32[]{:S(2)}) %copy-start.2) | copy-done | bytes 524312
  1.7 0.0 copy-start.3
  1.7 0.9 %copy-done.3 = bf16[128,512]{1,0:T(8,128)(2,1)S(1)} copy-done((bf16[128,512]{1,0:T(8,128)(2,1)S(1)}, bf16[128,512]{1,0:T(8,128)(2,1)}, u32[]{:S(2)}) %copy-start.3) | copy-done | bytes 131096
  2.6 0.0 copy-start.4
  2.6 0.7 %copy-done.4 = s32[512,1]{0,1:T(1,128)S(1)} copy-done((s32[512,1]{0,1:T(1,128)S(1)}, s32[512,1]{0,1:T(1,128)}, u32[]{:S(2)}) %copy-start.4) | copy-done | bytes 2072
  3.3 41.6 %shard_map.68.grad_ref = f32[512,512]{1,0:T(8,128)S(1)} custom-call(bf16[128,512]{1,0:T(8,128)(2,1)S(1)} %copy-done.3, bf16[512,512]{1,0:T(8,128)(2,1)S(1)} %copy-done.2, s32[1,512]{1,0:T(1,128)S(1)} %bitcast.1), custom_call_target="tpu_custom_call" | custom-call | tf_op jit(solution)/shard_map/pallas_call | solution.py:244
  44.9 0.0 copy-start
  44.9 1.6 %copy-done = f32[1,1,2,512,512]{4,3,2,1,0:T(8,128)S(1)} copy-done((f32[1,1,2,512,512]{4,3,2,1,0:T(8,128)S(1)}, f32[1,1,2,512,512]{4,3,2,1,0:T(8,128)}, u32[]{:S(2)}) %copy-start) | copy-done | bytes 2097176
  46.5 0.0 copy-start.1
  46.5 1.6 %copy-done.1 = f32[1,1,2,512,512]{4,3,2,1,0:T(8,128)S(1)} copy-done((f32[1,1,2,512,512]{4,3,2,1,0:T(8,128)S(1)}, f32[1,1,2,512,512]{4,3,2,1,0:T(8,128)}, u32[]{:S(2)}) %copy-start.1) | copy-done | bytes 2097176
  48.0 10.1 %shard_map.69 = (f32[512,512]{1,0:T(8,128)}, f32[1,1,2,512,512]{4,3,2,1,0:T(8,128)}) custom-call(f32[512,512]{1,0:T(8,128)S(1)} %shard_map.68.grad_ref, f32[1,1,2,512,512]{4,3,2,1,0:T(8,128)S(1)} %copy-done, f32[1,1,2,512,512]{4,3,2,1,0:T(8,128)S(1)} %copy-done.1), custom_call_target="tpu_custom_call" | custom-call | tf_op jit(solution)/shard_map/pallas_call | solution.py:353
Async XLA Ops:
  0.6 1.0 %copy-start.2 = (bf16[512,512]{1,0:T(8,128)(2,1)S(1)}, bf16[512,512]{1,0:T(8,128)(2,1)}, u32[]{:S(2)}) copy-start(bf16[512,512]{1,0:T(8,128)(2,1)} %cot_ref.1) | copy-start | bytes 1572868
  1.7 0.9 %copy-start.3 = (bf16[128,512]{1,0:T(8,128)(2,1)S(1)}, bf16[128,512]{1,0:T(8,128)(2,1)}, u32[]{:S(2)}) copy-start(bf16[128,512]{1,0:T(8,128)(2,1)} %acts_ref.1) | copy-start | bytes 393220
  2.6 0.7 %copy-start.4 = (s32[512,1]{0,1:T(1,128)S(1)}, s32[512,1]{0,1:T(1,128)}, u32[]{:S(2)}) copy-start(s32[512,1]{0,1:T(1,128)} %param.7) | copy-start | bytes 6148
  44.9 1.6 %copy-start = (f32[1,1,2,512,512]{4,3,2,1,0:T(8,128)S(1)}, f32[1,1,2,512,512]{4,3,2,1,0:T(8,128)}, u32[]{:S(2)}) copy-start(f32[1,1,2,512,512]{4,3,2,1,0:T(8,128)} %stats_ref.1) | copy-start | bytes 6291460
  46.5 1.6 %copy-start.1 = (f32[1,1,2,512,512]{4,3,2,1,0:T(8,128)S(1)}, f32[1,1,2,512,512]{4,3,2,1,0:T(8,128)}, u32[]{:S(2)}) copy-start(f32[1,1,2,512,512]{4,3,2,1,0:T(8,128)} %stale_ref.1) | copy-start | bytes 6291460

commit v2 on v1

v2 whole, which is shorter than its diff:
```python
import functools

import jax
import jax.numpy as jnp
from jax import lax
from jax.experimental import pallas as pl
from jax.experimental.pallas import tpu as pltpu
from jax.sharding import PartitionSpec as P

MESH = pl.DeviceIdType.MESH
F32 = jnp.float32
BF16 = jnp.bfloat16
B = 512
Q = 128
EXAMPLES = 128
MIB = 1 << 20


def contract(left, right, left_dim, right_dim):
    return lax.dot_general(
        left, right, (((left_dim,), (right_dim,)), ((), ())), preferred_element_type=F32
    )


class Names:
    def __init__(self):
        self.table = {}

    def __call__(self, *key):
        return self.table.setdefault(key, len(self.table))


COPIES = 96


def gather_kernel(
    acts_ref,
    cot_ref,
    ids_ref,
    stats_ref,
    stale_ref,
    grad_ref,
    stats_out,
    stale_out,
    acts_all,
    cot_all,
    ids_all,
    weights,
    local_sem,
    send_sem,
    recv_sem,
):
    role = lax.axis_index("role")
    fsdp = lax.axis_index("fsdp")
    dp = lax.axis_index("dp")
    z, core = fsdp // 2, fsdp % 2
    y, half = dp // 2, dp % 2
    number = Names()

    def device(role=role, z=z, core=core, y=y, half=half):
        return (role, z * 2 + core, y * 2 + half)

    across = device(half=1 - half)
    y_up, y_down = device(y=(y + 1) % 4), device(y=(y + 3) % 4)
    z_up, z_down = device(z=(z + 1) % 8), device(z=(z + 7) % 8)
    partner = device(role=1 - role)
    sibling = device(core=1 - core)
    row_peers = [(role, fsdp, (dp + step) % 8) for step in range(1, 8)]

    def acts_block(block_role, block_z, block_core):
        index = block_role * 16 + block_z * 2 + block_core
        return acts_all.at[index // 4, pl.ds(pl.multiple_of((index % 4) * Q, Q), Q)]

    def cot_part(block_y, block_half, quarter):
        return cot_all.at[block_y * 2 + block_half, pl.ds(quarter * Q, Q)]

    sent = []

    def copy_of(ref, key, target):
        index = number(*key)
        return pltpu.make_async_remote_copy(
            src_ref=ref,
            dst_ref=ref,
            send_sem=send_sem.at[index],
            recv_sem=recv_sem.at[index],
            device_id=target,
            device_id_type=MESH,
        )

    def send(ref, key, target):
        copy = copy_of(ref, key, target)
        copy.start()
        sent.append(copy)

    def arrived(ref, key):
        copy_of(ref, key, sibling).wait_recv()

    own_acts = acts_block(role, z, core)
    own_cot = cot_all.at[dp]
    local = [
        pltpu.make_async_copy(ids_ref, ids_all.at[dp], local_sem.at[0]),
        pltpu.make_async_copy(acts_ref, own_acts, local_sem.at[1]),
        pltpu.make_async_copy(cot_ref, own_cot, local_sem.at[2]),
    ]
    for copy in local:
        copy.start()

    barrier = pltpu.get_barrier_semaphore()
    others = [y_up, y_down, across] + [
        device(y=(y + 1) % 4, half=1 - half),
        device(y=(y + 3) % 4, half=1 - half),
        device(y=(y + 2) % 4),
        device(y=(y + 2) % 4, half=1 - half),
    ]
    everyone = others + [z_up, z_down, partner, sibling]
    for target in everyone:
        pl.semaphore_signal(barrier, inc=1, device_id=target, device_id_type=MESH)
    for copy in local:
        copy.wait()
    ahead = [
        pltpu.make_async_copy(stats_ref.at[0, 0], stats_out, local_sem.at[3]),
        pltpu.make_async_copy(stale_ref.at[0, 0], stale_out, local_sem.at[4]),
    ]
    for copy in ahead:
        copy.start()
    pl.semaphore_wait(barrier, len(everyone))

    for step, target in enumerate(row_peers, 1):
        send(ids_all.at[dp], ("ids", step), target)
    send(own_acts, ("partner",), partner)
    send(own_acts, ("up", 0, 1), z_up)
    send(own_acts, ("down", 0, 1), z_down)

    def own(quarter, direction):
        send(cot_part(y, half, quarter), ("y", direction, 0, quarter), y_up if direction else y_down)

    for pair in ((0, 3), (1, 2)):
        own(pair[0], 1)
        own(pair[1], 0)
        for quarter in pair:
            send(cot_part(y, half, quarter), ("x", 0, quarter), across)
    send(own_acts, ("sibling", 0, 0), sibling)

    for step in range(1, 8):
        arrived(ids_all.at[(dp + 8 - step) % 8], ("ids", step))

    def onehot(block):
        labels = lax.broadcasted_iota(jnp.int32, (EXAMPLES, B), 0)
        return jnp.where(ids_all[block] == labels, 1.0, 0.0)

    seen = lax.fori_loop(1, 8, lambda block, seen: seen + onehot(block), onehot(0))
    inverse = jnp.broadcast_to(1.0 / jnp.sum(seen, axis=1, keepdims=True), (EXAMPLES, Q))
    high = inverse.astype(BF16)
    rest = inverse - high.astype(F32)
    middle = rest.astype(BF16)
    low = (rest - middle.astype(F32)).astype(BF16)
    split = jnp.concatenate([high, middle, low], axis=1)

    def weigh(block, carry):
        spread = contract(onehot(block).astype(BF16), split, 0, 0)
        weights[block] = (spread[:, :Q] + spread[:, Q : 2 * Q]) + spread[:, 2 * Q :]
        return carry

    def step_acts(stream, hop):
        stream_role = role if stream == 0 else 1 - role
        for key, sign, target in (("up", -1, z_up), ("down", 1, z_down)):
            if hop == 4 and stream != (0 if key == "up" else 1):
                continue
            block = acts_block(stream_role, (z + 8 + sign * hop) % 8, core)
            arrived(block, (key, stream, hop))
            if hop < 3 or (hop == 3 and stream == (0 if key == "up" else 1)):
                send(block, (key, stream, hop + 1), target)
            send(block, ("sibling", stream, (8 + sign * hop) % 8), sibling)

    def from_sibling(offset):
        for stream in range(2):
            stream_role = role if stream == 0 else 1 - role
            arrived(acts_block(stream_role, (z + offset) % 8, 1 - core), ("sibling", stream, offset))

    up_y, down_y, far_y = (y + 1) % 4, (y + 3) % 4, (y + 2) % 4

    def pass_on(first, second):
        part = cot_part(down_y, half, first)
        arrived(part, ("y", 1, 0, first))
        send(part, ("y", 1, 1, first), y_up)
        part = cot_part(up_y, half, second)
        arrived(part, ("y", 0, 0, second))
        send(part, ("y", 0, 1, second), y_down)

    far = [copy_of(cot_part(far_y, half, quarter), ("x", 1, quarter), across) for quarter in (0, 3, 1, 2)]

    def send_far(*which):
        def start():
            for index in which:
                far[index].start()

        return start

    def far_arrived(*quarters):
        for quarter in quarters:
            arrived(cot_part(far_y, half, quarter), ("y", 1 if quarter < 2 else 0, 1, quarter))

    pass_on(0, 3)
    block = acts_block(1 - role, z, core)
    arrived(block, ("partner",))
    send(block, ("up", 1, 1), z_up)
    send(block, ("down", 1, 1), z_down)
    send(block, ("sibling", 1, 0), sibling)
    step_acts(0, 1)
    pass_on(1, 2)
    for quarter in (2, 3):
        own(quarter, 1)
        own(3 - quarter, 0)

    step_acts(1, 1)
    far_arrived(0, 3)
    send_far(0, 1)()
    far_arrived(1, 2)
    send_far(2, 3)()
    step_acts(0, 2)
    for quarter in (0, 3, 1):
        part = cot_part(y, 1 - half, quarter)
        arrived(part, ("x", 0, quarter))
        send(part, ("y", 1, 2, quarter), y_up)
        send(part, ("y", 0, 2, quarter), y_down)
    arrived(cot_part(y, 1 - half, 2), ("x", 0, 2))
    arrived(cot_part(down_y, half, 2), ("y", 1, 0, 2))
    send(
        cot_part(y, 1 - half, 2),
        ("y", 1, 2, 2),
        y_up,
    )
    send(
        cot_part(y, 1 - half, 2),
        ("y", 0, 2, 2),
        y_down,
    )
    step_acts(1, 2)
    lax.fori_loop(0, 8, weigh, 0)
    step_acts(0, 3)

    def wait_y(quarter):
        arrived(cot_part(down_y, 1 - half, quarter), ("y", 1, 2, quarter))
        arrived(cot_part(up_y, 1 - half, quarter), ("y", 0, 2, quarter))

    wait_y(0)
    step_acts(1, 3)

    arrived(cot_part(down_y, half, 3), ("y", 1, 0, 3))
    for quarter in (0, 1):
        arrived(cot_part(up_y, half, quarter), ("y", 0, 0, quarter))

    def scaled(block, rows):
        weight = weights[block, rows]
        return jnp.concatenate(
            [
                (cot_all[block, rows, pl.ds(lane, Q)].astype(F32) * weight).astype(BF16)
                for lane in range(0, B, Q)
            ],
            axis=1,
        )

    def early(index, carry):
        block_z = (z + index // 2 + 5) % 8
        block = index % 2 * 4 + block_z // 2
        rows = pl.ds(pl.multiple_of(block_z % 2 * (2 * Q), 2 * Q), 2 * Q)

        @pl.when(jnp.logical_or(block % 2 == half, block // 2 == y))
        def _():
            grad_ref[...] += contract(acts_all[block, rows], scaled(block, rows), 0, 0)

        return carry

    grad_ref[...] = jnp.zeros((B, B), F32)
    for offset in range(8):
        if offset != 4:
            from_sibling(offset)
    lax.fori_loop(0, 14, early, 0)
    step_acts(0, 4)
    step_acts(1, 4)
    from_sibling(4)
    lax.fori_loop(14, 16, early, 0)

    late = [block_y * 2 + 1 - half for block_y in (down_y, up_y, far_y)]
    for quarter in (0, 3, 1, 2):
        if quarter != 0:
            wait_y(quarter)
        arrived(cot_part(far_y, 1 - half, quarter), ("x", 1, quarter))
        rows = pl.ds(quarter * Q, Q)
        grad_ref[...] += contract(
            jnp.concatenate([acts_all[block, rows] for block in late], axis=0),
            jnp.concatenate([scaled(block, rows) for block in late], axis=0),
            0,
            0,
        )

    for copy in ahead:
        copy.wait()
    for copy in sent + far:
        copy.wait_send()
    assert len(number.table) <= COPIES


def gather(*operands):
    operands = [pltpu.with_memory_space_constraint(operand, pltpu.HBM) for operand in operands]
    return pl.pallas_call(
        gather_kernel,
        out_shape=(
            pltpu.VMEM((B, B), F32),
            pltpu.VMEM((2, B, B), F32),
            pltpu.VMEM((2, B, B), F32),
        ),
        in_specs=[pl.BlockSpec(memory_space=pltpu.HBM)] * 5,
        out_specs=(pl.BlockSpec(memory_space=pltpu.VMEM),) * 3,
        scratch_shapes=[
            pltpu.VMEM((8, B, B), BF16),
            pltpu.VMEM((8, B, B), BF16),
            pltpu.VMEM((8, 1, B), jnp.int32),
            pltpu.VMEM((8, B, Q), F32),
            pltpu.SemaphoreType.DMA((5,)),
            pltpu.SemaphoreType.DMA((COPIES,)),
            pltpu.SemaphoreType.DMA((COPIES,)),
        ],
        compiler_params=pltpu.CompilerParams(
            collective_id=0, has_side_effects=True, vmem_limit_bytes=24 * MIB
        ),
    )(*operands)


def parts_of(matrix):
    high = matrix.astype(BF16)
    return high, (matrix - high.astype(F32)).astype(BF16)


def precise(left, right, left_dim, right_dim):
    (left_high, left_low), (right_high, right_low) = left, right
    return contract(
        jnp.concatenate([left_high, left_low, left_high], axis=left_dim),
        jnp.concatenate([right_high, right_high, right_low], axis=right_dim),
        left_dim,
        right_dim,
    )


def rough(left, right):
    return contract(left.astype(BF16), right.astype(BF16), 1, 0)


def total(matrix):
    return jnp.sum(jnp.sum(matrix, axis=0, keepdims=True), axis=1, keepdims=True)


def block_kernel(
    grad, stats, stale, update_ref, new_ref, fresh, update, store_sem
):
    role = lax.axis_index("role")
    stores = [
        pltpu.make_async_copy(fresh.at[0], new_ref.at[0, 0, 0], store_sem.at[0]),
        pltpu.make_async_copy(fresh.at[1], new_ref.at[0, 0, 1], store_sem.at[1]),
    ]
    whole = grad[...]
    halves = parts_of(whole)
    for side in range(2):
        gram = contract(halves[0], halves[0], 1 - side, 1 - side)
        fresh[side] = 0.9 * stats[side] + (1.0 - 0.9) * gram
        stores[side].start()

    @pl.when(role == 0)
    def _():
        inner = precise(parts_of(stale[0]), halves, 1, 0)
        update[...] = precise(parts_of(inner), parts_of(stale[1]), 1, 0)

    @pl.when(role == 1)
    def _():
        sides = range(2)
        a = [fresh[side].astype(BF16) for side in sides]
        square = [total(fresh[side] * fresh[side]) for side in sides]
        r = [lax.rsqrt(square[side]) for side in sides]
        m2 = [(r[side] * r[side]) * rough(a[side], a[side]) for side in sides]
        m3 = [r[side] * rough(a[side], m2[side]) for side in sides]
        m4 = [(1.0 / 256) * m2[side] - (20.0 / 256) * r[side] * fresh[side] for side in sides]
        n = [
            (625.0 / 256) * r[side] * fresh[side]
            - (500.0 / 256) * m2[side]
            + (150.0 / 256) * m3[side]
            + rough(m3[side], m4[side])
            for side in sides
        ]
        n2 = [rough(n[side], n[side]) for side in sides]
        n3 = [rough(n[side], n2[side]) for side in sides]
        n4 = [
            (250.0 / 4096) * n[side] - (25.0 / 4096) * n2[side] + (1.0 / 4096) * n3[side] for side in sides
        ]
        g = [
            (-5.0 / 16 - 3125.0 / 4096) * n[side]
            + (3125.0 / 4096) * n2[side]
            - (1250.0 / 4096) * n3[side]
            + rough(n3[side], n4[side])
            for side in sides
        ]
        apart = [
            1.25 * g[side] - r[side] * ((25.0 / 64) * fresh[side] + 0.25 * rough(a[side], g[side]))
            for side in sides
        ]
        scale = [lax.rsqrt(jnp.sqrt(jnp.sqrt(value))) for value in square]
        inner = (125.0 / 64) * grad[...] + rough(apart[0], grad[...])
        product = (125.0 / 64) * inner + rough(inner, apart[1])
        update[...] = product * (scale[0] * scale[1])

    grad_size = jnp.sqrt(total(grad[...] * grad[...]) * (1.0 / (B * B)))
    prod_size = jnp.sqrt(total(update[...] * update[...]) * (1.0 / (B * B)) + 1e-06)
    ratio = grad_size / prod_size
    for part in range(4):
        rows = pl.ds(part * Q, Q)
        update[rows] = update[rows] * ratio
        copy = pltpu.make_async_copy(update.at[rows], update_ref.at[rows], store_sem.at[2 + part])
        copy.start()
        stores.append(copy)
    for copy in stores:
        copy.wait()


def block_step(grad, stats_old, stale_roots):
    return pl.pallas_call(
        block_kernel,
        out_shape=(
            jax.ShapeDtypeStruct((B, B), F32),
            jax.ShapeDtypeStruct((1, 1, 2, B, B), F32),
        ),
        in_specs=[pl.BlockSpec(memory_space=pltpu.VMEM)] * 3,
        out_specs=(pl.BlockSpec(memory_space=pl.ANY),) * 2,
        scratch_shapes=[
            pltpu.VMEM((2, B, B), F32),
            pltpu.VMEM((B, B), F32),
            pltpu.SemaphoreType.DMA((6,)),
        ],
        compiler_params=pltpu.CompilerParams(vmem_limit_bytes=32 * MIB),
    )(grad, stats_old, stale_roots)


def shards(acts, cotangent, example_of, stats_old, stale_roots):
    return block_step(*gather(acts, cotangent, example_of.reshape(1, B), stats_old, stale_roots))


def solution(mesh):
    return jax.shard_map(
        shards,
        mesh=mesh,
        in_specs=(
            P(("role", "fsdp"), "dp"),
            P("dp", ("role", "fsdp")),
            P("dp", None),
            P("dp", ("role", "fsdp"), None, None, None),
            P("dp", "fsdp", None, None, None),
        ),
        out_specs=(P("dp", ("role", "fsdp")), P("dp", ("role", "fsdp"), None, None, None)),
        check_vma=False,
    )
```

time: 58.5 us -> 49.9 us (0.85); the launches traced: 58.3 us -> 49 us
  local copies, waits for them, and re-layouts: 5.8 us -> 0 us
  Pallas kernels: 51.7 us -> 48.4 us
    unnamed x10 -> x0, local copies, waits for them, and re-layouts: 5.8 us -> none
    pallas_call x1, Pallas kernels: 10.1 us -> 7.39 us  [block_step(): pl.pallas_call(block_kernel, out_shape=(jax.ShapeDtypeStruct((B, B), F32)...]
    pallas_call x1, Pallas kernels: 41.6 us -> 41 us  [gather(): pl.pallas_call(gather_kernel, out_shape=(pltpu.VMEM((B, B), F32), pltpu.V...]
where the time goes in v2:
time: 49.9 us; the launch traced here: 49 us
  Pallas kernels  48.4 us (97%)
  between operations  0.64 us (1%)
    pallas_call x1, Pallas kernels, gather(): pl.pallas_call(gather_kernel, out_shape=(pltpu.VMEM((B, B), F32), pltpu.V...  41 us
    pallas_call x1, Pallas kernels, block_step(): pl.pallas_call(block_kernel, out_shape=(jax.ShapeDtypeStruct((B, B), F32)...  7.39 us

profile of v2, /device:TPU:3, one launch (start us, length us, event | category | flops | bytes accessed | tf_op | source)
XLA Modules:
  0.0 49.0 jit_solution(18400583069104178532)
XLA Ops:
  0.6 41.0 %shard_map.68 = (f32[512,512]{1,0:T(8,128)S(1)}, f32[2,512,512]{2,1,0:T(8,128)S(1)}, f32[2,512,512]{2,1,0:T(8,128)S(1)}) custom-call(bf16[128,512]{1,0:T(8,128)(2,1)} %acts_ref.1, bf16[512,512]{1,0:T(8,128)(2,1)} %cot_ref.1, s32[1,512]{1,0:T(1,128)} %bitcast.1, f32[1,1,2,512,512]{4,3,2,1,0:T(8,128)} %stats_ref.1, f32[1,1,2,512,512]{4,3,2,1,0:T(8,128)} %stale_ref.1), custom_call_target="tpu_custom_call" | custom-call | tf_op jit(solution)/shard_map/pallas_call | solution.py:306
  41.6 7.4 %shard_map.69 = (f32[512,512]{1,0:T(8,128)}, f32[1,1,2,512,512]{4,3,2,1,0:T(8,128)}) custom-call(f32[512,512]{1,0:T(8,128)S(1)} %get-tuple-element.5.grad, f32[2,512,512]{2,1,0:T(8,128)S(1)} %get-tuple-element.6.stats, f32[2,512,512]{2,1,0:T(8,128)S(1)} %get-tuple-element.7.stale), custom_call_target="tpu_custom_call" | custom-call | tf_op jit(solution)/shard_map/pallas_call | solution.py:424

commit v3 on v2

--- a/solution.py
+++ b/solution.py
@@ -237,14 +237,8 @@
     )
     step_acts(1, 2)
     lax.fori_loop(0, 8, weigh, 0)
+    grad_ref[...] = jnp.zeros((B, B), F32)
     step_acts(0, 3)
-
-    def wait_y(quarter):
-        arrived(cot_part(down_y, 1 - half, quarter), ("y", 1, 2, quarter))
-        arrived(cot_part(up_y, 1 - half, quarter), ("y", 0, 2, quarter))
-
-    wait_y(0)
-    step_acts(1, 3)
 
     arrived(cot_part(down_y, half, 3), ("y", 1, 0, 3))
     for quarter in (0, 1):
@@ -260,32 +254,67 @@
             axis=1,
         )
 
-    def early(index, carry):
-        block_z = (z + index // 2 + 5) % 8
-        block = index % 2 * 4 + block_z // 2
-        rows = pl.ds(pl.multiple_of(block_z % 2 * (2 * Q), 2 * Q), 2 * Q)
-
-        @pl.when(jnp.logical_or(block % 2 == half, block // 2 == y))
-        def _():
-            grad_ref[...] += contract(acts_all[block, rows], scaled(block, rows), 0, 0)
-
-        return carry
-
-    grad_ref[...] = jnp.zeros((B, B), F32)
-    for offset in range(8):
-        if offset != 4:
-            from_sibling(offset)
-    lax.fori_loop(0, 14, early, 0)
+    def pair_distance(block):
+        return (block % 4 * 2 + 8 - z // 2 * 2) % 8
+
+    def stage(block):
+        begin = pair_distance(block)
+        odd = z % 2
+        return jnp.where(begin == 4, 2, jnp.where(begin == 2 + 4 * odd, 1, 0))
+
+    def early(want):
+        def one(index, carry):
+            block = (y + index % 4) % 4 * 2 + (half + index // 4) % 2
+
+            @pl.when(stage(block) == want)
+            def _():
+                grad_ref[...] += contract(acts_all[block], scaled(block, pl.ds(0, B)), 0, 0)
+
+            return carry
+
+        lax.fori_loop(0, 5, one, 0)
+
+    def outer(last):
+        def one(index, carry):
+            block = (y + 1 + index) % 4 * 2 + 1 - half
+            rows = [pl.ds(0, Q), pl.ds(3 * Q, Q)]
+
+            @pl.when((stage(block) == 2) == last)
+            def _():
+                grad_ref[...] += contract(
+                    jnp.concatenate([acts_all[block, part] for part in rows], axis=0),
+                    jnp.concatenate([scaled(block, part) for part in rows], axis=0),
+                    0,
+                    0,
+                )
+
+            return carry
+
+        lax.fori_loop(0, 3, one, 0)
+
+    def wave_arrived(quarter):
+        arrived(cot_part(down_y, 1 - half, quarter), ("y", 1, 2, quarter))
+        arrived(cot_part(up_y, 1 - half, quarter), ("y", 0, 2, quarter))
+        arrived(cot_part(far_y, 1 - half, quarter), ("x", 1, quarter))
+
+    late = [block_y * 2 + 1 - half for block_y in (up_y, far_y, down_y)]
+    for offset in (0, 1, 7, 2, 6):
+        from_sibling(offset)
+    early(0)
+    step_acts(1, 3)
+    from_sibling(3)
+    from_sibling(5)
+    early(1)
+    wave_arrived(0)
+    wave_arrived(3)
+    outer(False)
     step_acts(0, 4)
     step_acts(1, 4)
     from_sibling(4)
-    lax.fori_loop(14, 16, early, 0)
-
-    late = [block_y * 2 + 1 - half for block_y in (down_y, up_y, far_y)]
-    for quarter in (0, 3, 1, 2):
-        if quarter != 0:
-            wait_y(quarter)
-        arrived(cot_part(far_y, 1 - half, quarter), ("x", 1, quarter))
+    early(2)
+    outer(True)
+    for quarter in (1, 2):
+        wave_arrived(quarter)
         rows = pl.ds(quarter * Q, Q)
         grad_ref[...] += contract(
             jnp.concatenate([acts_all[block, rows] for block in late], axis=0),
@@ -350,25 +379,28 @@
     return jnp.sum(jnp.sum(matrix, axis=0, keepdims=True), axis=1, keepdims=True)
 
 
-def block_kernel(
-    grad, stats, stale, update_ref, new_ref, fresh, update, store_sem
-):
+def block_kernel(grad, stats, stale, update_ref, new_ref, fresh, update, ratio, store_sem):
     role = lax.axis_index("role")
     stores = [
         pltpu.make_async_copy(fresh.at[0], new_ref.at[0, 0, 0], store_sem.at[0]),
         pltpu.make_async_copy(fresh.at[1], new_ref.at[0, 0, 1], store_sem.at[1]),
     ]
-    whole = grad[...]
-    halves = parts_of(whole)
+    rounded = grad[...].astype(BF16)
     for side in range(2):
-        gram = contract(halves[0], halves[0], 1 - side, 1 - side)
+        gram = contract(rounded, rounded, 1 - side, 1 - side)
         fresh[side] = 0.9 * stats[side] + (1.0 - 0.9) * gram
         stores[side].start()
+    grad_size = jnp.sqrt(total(grad[...] * grad[...]) * (1.0 / (B * B)))
+
+    def finish(product, scale):
+        update[...] = product
+        square = total(product * product) * (1.0 / (B * B))
+        ratio[...] = grad_size * scale / jnp.sqrt(square * (scale * scale) + 1e-06)
 
     @pl.when(role == 0)
     def _():
-        inner = precise(parts_of(stale[0]), halves, 1, 0)
-        update[...] = precise(parts_of(inner), parts_of(stale[1]), 1, 0)
+        inner = precise(parts_of(stale[0]), parts_of(grad[...]), 1, 0)
+        finish(precise(parts_of(inner), parts_of(stale[1]), 1, 0), jnp.ones((1, 1), F32))
 
     @pl.when(role == 1)
     def _():
@@ -376,43 +408,32 @@
         a = [fresh[side].astype(BF16) for side in sides]
         square = [total(fresh[side] * fresh[side]) for side in sides]
         r = [lax.rsqrt(square[side]) for side in sides]
-        m2 = [(r[side] * r[side]) * rough(a[side], a[side]) for side in sides]
-        m3 = [r[side] * rough(a[side], m2[side]) for side in sides]
-        m4 = [(1.0 / 256) * m2[side] - (20.0 / 256) * r[side] * fresh[side] for side in sides]
+        u = [
+            ((r[side] * r[side]) * rough(a[side], a[side]) - (10.0 * r[side]) * fresh[side]).astype(BF16)
+            for side in sides
+        ]
+        w = [50.0 * u[side].astype(F32) + rough(u[side], u[side]) for side in sides]
         n = [
-            (625.0 / 256) * r[side] * fresh[side]
-            - (500.0 / 256) * m2[side]
-            + (150.0 / 256) * m3[side]
-            + rough(m3[side], m4[side])
-            for side in sides
+            (r[side] * (1.0 / 256)) * (625.0 * fresh[side] + rough(a[side], w[side])) for side in sides
         ]
         n2 = [rough(n[side], n[side]) for side in sides]
         n3 = [rough(n[side], n2[side]) for side in sides]
-        n4 = [
-            (250.0 / 4096) * n[side] - (25.0 / 4096) * n2[side] + (1.0 / 4096) * n3[side] for side in sides
-        ]
+        n4 = [250.0 * n[side] - 25.0 * n2[side] + n3[side] for side in sides]
         g = [
-            (-5.0 / 16 - 3125.0 / 4096) * n[side]
-            + (3125.0 / 4096) * n2[side]
-            - (1250.0 / 4096) * n3[side]
-            + rough(n3[side], n4[side])
+            3125.0 * n2[side] - (1280.0 + 3125.0) * n[side] - 1250.0 * n3[side] + rough(n3[side], n4[side])
             for side in sides
         ]
         apart = [
-            1.25 * g[side] - r[side] * ((25.0 / 64) * fresh[side] + 0.25 * rough(a[side], g[side]))
-            for side in sides
+            1.25 * g[side] - r[side] * (1600.0 * fresh[side] + 0.25 * rough(a[side], g[side])) for side in sides
         ]
         scale = [lax.rsqrt(jnp.sqrt(jnp.sqrt(value))) for value in square]
-        inner = (125.0 / 64) * grad[...] + rough(apart[0], grad[...])
-        product = (125.0 / 64) * inner + rough(inner, apart[1])
-        update[...] = product * (scale[0] * scale[1])
-
-    grad_size = jnp.sqrt(total(grad[...] * grad[...]) * (1.0 / (B * B)))
-    prod_size = jnp.sqrt(total(update[...] * update[...]) * (1.0 / (B * B)) + 1e-06)
-    ratio = grad_size / prod_size
+        inner = 8000.0 * grad[...] + rough(apart[0], grad[...])
+        product = 8000.0 * inner + rough(inner, apart[1])
+        finish(product, scale[0] * scale[1] * (1.0 / (4096.0 * 4096.0)))
+
     for part in range(4):
         rows = pl.ds(part * Q, Q)
-        update[rows] = update[rows] * ratio
+        update[rows] = update[rows] * ratio[...]
         copy = pltpu.make_async_copy(update.at[rows], update_ref.at[rows], store_sem.at[2 + part])
         copy.start()
         stores.append(copy)
@@ -432,6 +453,7 @@
         scratch_shapes=[
             pltpu.VMEM((2, B, B), F32),
             pltpu.VMEM((B, B), F32),
+            pltpu.VMEM((1, 1), F32),
             pltpu.SemaphoreType.DMA((6,)),
         ],
         compiler_params=pltpu.CompilerParams(vmem_limit_bytes=32 * MIB),

time: 49.9 us -> 48.3 us (0.968); the launches traced: 49 us -> 48.2 us
  Pallas kernels: 48.4 us -> 47.6 us
    pallas_call x1, Pallas kernels: 41 us -> 40.2 us  [gather(): pl.pallas_call(gather_kernel, out_shape=(pltpu.VMEM((B, B), F32), pltpu.V...]
where the time goes in v3:
time: 48.3 us; the launch traced here: 48.2 us
  Pallas kernels  47.6 us (99%)
  between operations  0.64 us (1%)
    pallas_call x1, Pallas kernels, gather(): pl.pallas_call(gather_kernel, out_shape=(pltpu.VMEM((B, B), F32), pltpu.V...  40.2 us
    pallas_call x1, Pallas kernels, block_step(): pl.pallas_call(block_kernel, out_shape=(jax.ShapeDtypeStruct((B, B), F32)...  7.42 us

profile of v3, /device:TPU:3, one launch (start us, length us, event | category | flops | bytes accessed | tf_op | source)
XLA Modules:
  0.0 48.2 jit_solution(15670648849355374876)
XLA Ops:
  0.6 40.2 %shard_map.68 = (f32[512,512]{1,0:T(8,128)S(1)}, f32[2,512,512]{2,1,0:T(8,128)S(1)}, f32[2,512,512]{2,1,0:T(8,128)S(1)}) custom-call(bf16[128,512]{1,0:T(8,128)(2,1)} %acts_ref.1, bf16[512,512]{1,0:T(8,128)(2,1)} %cot_ref.1, s32[1,512]{1,0:T(1,128)} %bitcast.1, f32[1,1,2,512,512]{4,3,2,1,0:T(8,128)} %stats_ref.1, f32[1,1,2,512,512]{4,3,2,1,0:T(8,128)} %stale_ref.1), custom_call_target="tpu_custom_call" | custom-call | tf_op jit(solution)/shard_map/pallas_call | solution.py:335
  40.8 7.4 %shard_map.69 = (f32[512,512]{1,0:T(8,128)}, f32[1,1,2,512,512]{4,3,2,1,0:T(8,128)}) custom-call(f32[512,512]{1,0:T(8,128)S(1)} %get-tuple-element.5.grad, f32[2,512,512]{2,1,0:T(8,128)S(1)} %get-tuple-element.6.stats, f32[2,512,512]{2,1,0:T(8,128)S(1)} %get-tuple-element.7.stale), custom_call_target="tpu_custom_call" | custom-call | tf_op jit(solution)/shard_map/pallas_call | solution.py:445

commit v4 on v3

--- a/solution.py
+++ b/solution.py
@@ -13,6 +13,7 @@
 B = 512
 Q = 128
 EXAMPLES = 128
+REST = 48
 MIB = 1 << 20
 
 
@@ -74,6 +75,12 @@
     def cot_part(block_y, block_half, quarter):
         return cot_all.at[block_y * 2 + block_half, pl.ds(quarter * Q, Q)]
 
+    def head_of(block_y, block_half):
+        return cot_all.at[block_y * 2 + block_half, pl.ds(2 * Q, Q - REST)]
+
+    def rest_of(block_y, block_half):
+        return cot_all.at[block_y * 2 + block_half, pl.ds(3 * Q - REST, REST)]
+
     sent = []
 
     def copy_of(ref, key, target):
@@ -225,16 +232,11 @@
         send(part, ("y", 0, 2, quarter), y_down)
     arrived(cot_part(y, 1 - half, 2), ("x", 0, 2))
     arrived(cot_part(down_y, half, 2), ("y", 1, 0, 2))
-    send(
-        cot_part(y, 1 - half, 2),
-        ("y", 1, 2, 2),
-        y_up,
-    )
-    send(
-        cot_part(y, 1 - half, 2),
-        ("y", 0, 2, 2),
-        y_down,
-    )
+    part = head_of(y, 1 - half)
+    send(part, ("y", 1, 2, 2), y_up)
+    send(part, ("y", 0, 2, 2), y_down)
+    send(rest_of(down_y, half), ("x", 2, 0), across)
+    send(rest_of(up_y, half), ("x", 2, 1), across)
     step_acts(1, 2)
     lax.fori_loop(0, 8, weigh, 0)
     grad_ref[...] = jnp.zeros((B, B), F32)
@@ -293,8 +295,12 @@
         lax.fori_loop(0, 3, one, 0)
 
     def wave_arrived(quarter):
-        arrived(cot_part(down_y, 1 - half, quarter), ("y", 1, 2, quarter))
-        arrived(cot_part(up_y, 1 - half, quarter), ("y", 0, 2, quarter))
+        part_of = head_of if quarter == 2 else functools.partial(cot_part, quarter=quarter)
+        arrived(part_of(down_y, 1 - half), ("y", 1, 2, quarter))
+        arrived(part_of(up_y, 1 - half), ("y", 0, 2, quarter))
+        if quarter == 2:
+            arrived(rest_of(down_y, 1 - half), ("x", 2, 0))
+            arrived(rest_of(up_y, 1 - half), ("x", 2, 1))
         arrived(cot_part(far_y, 1 - half, quarter), ("x", 1, quarter))
 
     late = [block_y * 2 + 1 - half for block_y in (up_y, far_y, down_y)]

time: 48.3 us -> 48.3 us (level)
  no operation moved by 1% of the time
where the time goes in v4:
time: 48.3 us; the launch traced here: 48.2 us
  Pallas kernels  47.6 us (99%)
  between operations  0.64 us (1%)
    pallas_call x1, Pallas kernels, gather(): pl.pallas_call(gather_kernel, out_shape=(pltpu.VMEM((B, B), F32), pltpu.V...  40.2 us
    pallas_call x1, Pallas kernels, block_step(): pl.pallas_call(block_kernel, out_shape=(jax.ShapeDtypeStruct((B, B), F32)...  7.42 us

profile of v4, /device:TPU:3, one launch (start us, length us, event | category | flops | bytes accessed | tf_op | source)
XLA Modules:
  0.0 48.2 jit_solution(4194742037231886201)
XLA Ops:
  0.6 40.2 %shard_map.68 = (f32[512,512]{1,0:T(8,128)S(1)}, f32[2,512,512]{2,1,0:T(8,128)S(1)}, f32[2,512,512]{2,1,0:T(8,128)S(1)}) custom-call(bf16[128,512]{1,0:T(8,128)(2,1)} %acts_ref.1, bf16[512,512]{1,0:T(8,128)(2,1)} %cot_ref.1, s32[1,512]{1,0:T(1,128)} %bitcast.1, f32[1,1,2,512,512]{4,3,2,1,0:T(8,128)} %stats_ref.1, f32[1,1,2,512,512]{4,3,2,1,0:T(8,128)} %stale_ref.1), custom_call_target="tpu_custom_call" | custom-call | tf_op jit(solution)/shard_map/pallas_call | solution.py:341
  40.8 7.4 %shard_map.69 = (f32[512,512]{1,0:T(8,128)}, f32[1,1,2,512,512]{4,3,2,1,0:T(8,128)}) custom-call(f32[512,512]{1,0:T(8,128)S(1)} %get-tuple-element.5.grad, f32[2,512,512]{2,1,0:T(8,128)S(1)} %get-tuple-element.6.stats, f32[2,512,512]{2,1,0:T(8,128)S(1)} %get-tuple-element.7.stale), custom_call_target="tpu_custom_call" | custom-call | tf_op jit(solution)/shard_map/pallas_call | solution.py:451

commit v5 on v4

--- a/solution.py
+++ b/solution.py
@@ -218,6 +218,7 @@
     for quarter in (2, 3):
         own(quarter, 1)
         own(3 - quarter, 0)
+    lax.fori_loop(0, 8, weigh, 0)
 
     step_acts(1, 1)
     far_arrived(0, 3)
@@ -238,7 +239,6 @@
     send(rest_of(down_y, half), ("x", 2, 0), across)
     send(rest_of(up_y, half), ("x", 2, 1), across)
     step_acts(1, 2)
-    lax.fori_loop(0, 8, weigh, 0)
     grad_ref[...] = jnp.zeros((B, B), F32)
     step_acts(0, 3)
 
@@ -311,11 +311,11 @@
     from_sibling(3)
     from_sibling(5)
     early(1)
+    step_acts(0, 4)
+    step_acts(1, 4)
     wave_arrived(0)
     wave_arrived(3)
     outer(False)
-    step_acts(0, 4)
-    step_acts(1, 4)
     from_sibling(4)
     early(2)
     outer(True)

time: 48.3 us -> 48.2 us (level)
  no operation moved by 1% of the time
where the time goes in v5:
time: 48.2 us; the launch traced here: 48.1 us
  Pallas kernels  47.4 us (98%)
  between operations  0.64 us (1%)
    pallas_call x1, Pallas kernels, gather(): pl.pallas_call(gather_kernel, out_shape=(pltpu.VMEM((B, B), F32), pltpu.V...  40 us
    pallas_call x1, Pallas kernels, block_step(): pl.pallas_call(block_kernel, out_shape=(jax.ShapeDtypeStruct((B, B), F32)...  7.42 us

profile of v5, /device:TPU:3, one launch (start us, length us, event | category | flops | bytes accessed | tf_op | source)
XLA Modules:
  0.0 48.1 jit_solution(12652621669873245891)
XLA Ops:
  0.6 40.0 %shard_map.68 = (f32[512,512]{1,0:T(8,128)S(1)}, f32[2,512,512]{2,1,0:T(8,128)S(1)}, f32[2,512,512]{2,1,0:T(8,128)S(1)}) custom-call(bf16[128,512]{1,0:T(8,128)(2,1)} %acts_ref.1, bf16[512,512]{1,0:T(8,128)(2,1)} %cot_ref.1, s32[1,512]{1,0:T(1,128)} %bitcast.1, f32[1,1,2,512,512]{4,3,2,1,0:T(8,128)} %stats_ref.1, f32[1,1,2,512,512]{4,3,2,1,0:T(8,128)} %stale_ref.1), custom_call_target="tpu_custom_call" | custom-call | tf_op jit(solution)/shard_map/pallas_call | solution.py:341
  40.7 7.4 %shard_map.69 = (f32[512,512]{1,0:T(8,128)}, f32[1,1,2,512,512]{4,3,2,1,0:T(8,128)}) custom-call(f32[512,512]{1,0:T(8,128)S(1)} %get-tuple-element.5.grad, f32[2,512,512]{2,1,0:T(8,128)S(1)} %get-tuple-element.6.stats, f32[2,512,512]{2,1,0:T(8,128)S(1)} %get-tuple-element.7.stale), custom_call_target="tpu_custom_call" | custom-call | tf_op jit(solution)/shard_map/pallas_call | solution.py:451
